TPU v7x, 128 devices: a whole 4x4x4 slice. The times are simulated.
128 devices in a mesh: face: 8 (over z_lo, x), tile: 16 (over z_hi, y, core).
Axes of the slice: x: 4, y: 4, z: 4 (z_hi: 2, z_lo: 2; z = z_hi * 2 + z_lo), core: 2. Of those that a mesh axis runs over, the one named last changes fastest.
Arguments:
- source: bfloat16 [8192, 16, 128], P(('face', 'tile')), may hold values from -6 to 6
- entry_block: int32 [16384], P(('face', 'tile')), may hold values from 0 to 16383, as said below
- entry_source: int32 [16384], P(('face', 'tile')), may hold values from 0 to 63
- entry_weight: bfloat16 [16384, 128, 128], P(('face', 'tile')), may hold values from -0.5 to 0.5
- lat_to_nested: int32 [16384], P(('face', 'tile')), may hold values from 0 to 16383, as said below
- face_links: int32 [8, 4, 3], replicated, may hold values from 0 to 7, as said below
- w_in: bfloat16 [16, 90], replicated, may hold values from -1.5 to 1.5
- b_in: float32 [90], replicated, may hold values from -3 to 3
- kernel: float32 [9, 90], replicated, may hold values from -2 to 2
- ln_gain: float32 [90], replicated, may hold values from 0.1 to 1.9
- ln_bias: float32 [90], replicated, may hold values from -3 to 3
- w_one: bfloat16 [90, 360], replicated, may hold values from -0.625 to 0.625
- b_one: float32 [360], replicated, may hold values from -3 to 3
- w_two: bfloat16 [360, 90], replicated, may hold values from -0.3125 to 0.3125
- b_two: float32 [90], replicated, may hold values from -3 to 3
- cotangent: bfloat16 [8, 90, 512, 512], P('face', None, 'tile'), may hold values from -6 to 6
Outputs:
- output: bfloat16 [8, 90, 512, 512], P('face', None, 'tile')
- grad_one: float32 [90, 360], replicated
- grad_two: float32 [360, 90], replicated
- grad_kernel: float32 [9, 90], replicated
Inputs may be any that keep to these rules, and one draw needn't show every extreme that they name: `entry_block`: blocks k * 128 to (k + 1) * 128 - 1 belong to device k. At most 2 entries of one device name blocks of one device; in every draw one device gets exactly 2 from every device. `lat_to_nested`: A permutation of all blocks; the 128 blocks of each device go one to each device. `face_links`: entry [f, s, 0] names a face other than f; [f, s, 1] a side 0 to 3; [f, s, 2] is 0 or 1.
All inputs are finite; a program needn't handle non-finite values.
Results may differ from a plain program's by a relative error of at most 0.0081.
Values may be sent and summed in bfloat16 or wider, within the bound.
A program may use at most 192 MiB of HBM per device.

v0:
```python
import math
import jax
import jax.numpy as jnp
from jax import lax
from jax.sharding import PartitionSpec as P

CAP = 2
GELU_K = 0.7978845608028654
GELU_C = 0.044715
NORM_EPS = 1e-06


def with_halo(cells, sides, width):
    for axis, dim in sides:
        count = lax.axis_size(axis)
        ends = count - 1
        head = lax.slice_in_dim(cells, 0, width, axis=dim)
        tail = lax.slice_in_dim(cells, cells.shape[dim] - width, cells.shape[dim], axis=dim)
        cells = jnp.concatenate(
            [
                lax.ppermute(tail, axis, [(i, (i + 1) % count) for i in range(ends)]),
                cells,
                lax.ppermute(head, axis, [((i + 1) % count, i) for i in range(ends)]),
            ],
            axis=dim,
        )
    return cells


def gelu_pair(pre_act):
    inner = GELU_K * (pre_act + GELU_C * pre_act * pre_act * pre_act)
    tanh_val = jnp.tanh(inner)
    gelu_val = 0.5 * pre_act * (1.0 + tanh_val)
    gelu_slope = 0.5 * (1.0 + tanh_val) + 0.5 * pre_act * (1.0 - tanh_val * tanh_val) * GELU_K * (
        1.0 + 3.0 * GELU_C * pre_act * pre_act
    )
    return (gelu_val, gelu_slope)


def contract_rows(left_mat, right_mat):
    return lax.dot_general(
        left_mat, right_mat, (((1,), (1,)), ((), ())), preferred_element_type=jnp.float32
    )


def strip_work(padded, middle, cotan, kernel, ln_gain, ln_bias, w_one, b_one, w_two, b_two, scale):
    lat_count = padded.shape[0]
    row_count = padded.shape[1] - 2
    col_count = padded.shape[2] - 2
    wide = padded.astype(jnp.float32)
    depth_sum = jnp.zeros((lat_count, row_count, col_count), jnp.float32)
    for tap_index in range(9):
        row_off = tap_index // 3
        col_off = tap_index % 3
        window = wide[:, row_off : row_off + row_count, col_off : col_off + col_count]
        depth_sum = depth_sum + kernel[tap_index][:, None, None] * window
    flat = depth_sum.reshape(lat_count, row_count * col_count)
    mean_val = jnp.mean(flat, axis=0, keepdims=True)
    centered = flat - mean_val
    variance = jnp.mean(centered * centered, axis=0, keepdims=True)
    inv_std = lax.rsqrt(variance + NORM_EPS)
    scaled = centered * inv_std
    normed = (scaled * ln_gain[:, None] + ln_bias[:, None]).astype(jnp.bfloat16)
    pre_act = jnp.dot(w_one.T, normed, preferred_element_type=jnp.float32) + b_one[:, None]
    gelu_val, gelu_slope = gelu_pair(pre_act)
    hidden = gelu_val.astype(jnp.bfloat16)
    summed = (
        jnp.dot(w_two.T, hidden, preferred_element_type=jnp.float32)
        + b_two[:, None]
        + middle.reshape(lat_count, -1).astype(jnp.float32)
    )
    output = summed.astype(jnp.bfloat16).reshape(lat_count, row_count, col_count)
    cot_flat = cotan.reshape(lat_count, -1)
    grad_two = contract_rows(hidden, cot_flat) * scale
    back_hidden = jnp.dot(w_two, cot_flat, preferred_element_type=jnp.float32)
    back_pre = (back_hidden * gelu_slope).astype(jnp.bfloat16)
    grad_one = contract_rows(normed, back_pre) * scale
    back_hat = jnp.dot(w_one, back_pre, preferred_element_type=jnp.float32) * ln_gain[:, None]
    back_depth = inv_std * (
        back_hat
        - jnp.mean(back_hat, axis=0, keepdims=True)
        - scaled * jnp.mean(back_hat * scaled, axis=0, keepdims=True)
    )
    back_grid = back_depth.reshape(lat_count, row_count, col_count)
    kernel_rows = []
    for tap_index in range(9):
        row_off = tap_index // 3
        col_off = tap_index % 3
        window = wide[:, row_off : row_off + row_count, col_off : col_off + col_count]
        kernel_rows.append(jnp.sum(back_grid * window, axis=(1, 2)))
    grad_kernel = jnp.stack(kernel_rows, axis=0) * scale
    return (output, grad_one, grad_two, grad_kernel)


def lift(w_in, b_in, values):
    flat = values.reshape(values.shape[0], -1)
    mixed = jnp.dot(w_in.T, flat, preferred_element_type=jnp.float32) + b_in[:, None]
    return mixed.astype(jnp.bfloat16).reshape((w_in.shape[1],) + values.shape[1:])


def assemble(rows_part, cols_part):
    tile_count = rows_part.shape[0]
    chan_count = rows_part.shape[1]
    left_line = cols_part[:, 0].transpose(1, 0, 2).reshape(chan_count, -1)
    right_line = cols_part[:, 1].transpose(1, 0, 2).reshape(chan_count, -1)
    return jnp.stack([rows_part[0], rows_part[tile_count - 1], left_line, right_line], axis=0)


def per_device(
    source,
    entry_block,
    entry_source,
    entry_weight,
    lat_to_nested,
    face_links,
    w_in,
    b_in,
    kernel,
    ln_gain,
    ln_bias,
    w_one,
    b_one,
    w_two,
    b_two,
    cotangent,
):
    tile_count = lax.axis_size("tile")
    tile_at = lax.axis_index("tile")
    face_at = lax.axis_index("face")
    face_count = lax.axis_size("face")
    dev_count = lax.axis_size(("face", "tile"))
    in_count = source.shape[1]
    block_len = entry_weight.shape[2]
    row_count = cotangent.shape[2]
    line_len = cotangent.shape[3]
    chosen = jnp.take(source, entry_source, axis=0)
    partials = jnp.einsum(
        "eis,esp->eip", chosen, entry_weight, preferred_element_type=jnp.float32
    ).astype(jnp.bfloat16)
    owner_dev = entry_block // dev_count
    local_block = entry_block % dev_count
    hit_table = (owner_dev[:, None] == jnp.arange(dev_count, dtype=jnp.int32)[None, :]).astype(
        jnp.int32
    )
    slot_rank = jnp.sum((jnp.cumsum(hit_table, axis=0) - 1) * hit_table, axis=1)
    outbox = (
        jnp.zeros((dev_count, CAP, in_count, block_len), jnp.bfloat16)
        .at[owner_dev, slot_rank]
        .set(partials)
    )
    labels = (
        jnp.full((dev_count, CAP), dev_count, jnp.int32).at[owner_dev, slot_rank].set(local_block)
    )
    received, got_labels = (
        lax.all_to_all(outbox, ("face", "tile"), split_axis=0, concat_axis=0, tiled=True),
        lax.all_to_all(labels, ("face", "tile"), split_axis=0, concat_axis=0, tiled=True),
    )
    lat_sum = jnp.zeros((dev_count, in_count, block_len), jnp.float32)
    lat_sum = lat_sum.at[got_labels.reshape(-1)].add(
        received.reshape(-1, in_count, block_len).astype(jnp.float32), mode="drop"
    )
    lat_field = lat_sum.astype(jnp.bfloat16)
    target_dev = lat_to_nested // dev_count
    target_spot = lat_to_nested % dev_count
    outgoing = jnp.zeros_like(lat_field).at[target_dev].set(lat_field)
    out_spots = jnp.zeros((dev_count,), jnp.int32).at[target_dev].set(target_spot)
    incoming, in_spots = (
        lax.all_to_all(outgoing, ("face", "tile"), split_axis=0, concat_axis=0, tiled=True),
        lax.all_to_all(out_spots, ("face", "tile"), split_axis=0, concat_axis=0, tiled=True),
    )
    placed = jnp.zeros_like(incoming).at[in_spots].set(incoming)
    inputs_tile = placed.transpose(1, 0, 2).reshape(in_count, row_count, line_len)
    latent = lift(w_in, b_in, inputs_tile)
    chan_count = latent.shape[0]
    row_start = tile_at * row_count
    edge_cols = jnp.stack([latent[:, :, 0], latent[:, :, line_len - 1]], axis=0)
    edge_row = jnp.where(tile_at == 0, latent[:, 0, :], latent[:, row_count - 1, :])
    rows_face, cols_face = (
        lax.all_gather(edge_row.reshape(-1), "tile", axis=0, tiled=True),
        lax.all_gather(edge_cols.reshape(-1), "tile", axis=0, tiled=True),
    )
    own_lines = assemble(
        rows_face.reshape(tile_count, chan_count, line_len),
        cols_face.reshape(tile_count, 2, chan_count, row_count),
    )
    all_lines = lax.all_gather(own_lines.reshape(-1), "face", axis=0, tiled=True).reshape(
        face_count, 4, chan_count, line_len
    )
    face_link = face_links[face_at]
    picked = all_lines[face_link[:, 0], face_link[:, 1]]
    picked = jnp.where(face_link[:, 2][:, None, None] == 1, picked[:, :, ::-1], picked)
    row_lines = picked[0:2]
    full_cols = jnp.pad(picked[2:4], ((0, 0), (0, 0), (1, 1)))
    side_cols = lax.dynamic_slice_in_dim(full_cols, row_start, row_count + 2, 2)
    rim = jnp.stack([latent[:, 0, :], latent[:, row_count - 1, :]], axis=1)
    extended = with_halo(rim, (("tile", 1),), 1)
    upper_row = extended[:, 0, :]
    lower_row = extended[:, 3, :]
    spot_ids = jnp.arange(row_count + 2, dtype=jnp.int32) + row_start - 1
    inside = (spot_ids >= 0) & (spot_ids < line_len)
    side_cols = jnp.where(inside[None, None, :], side_cols, jnp.zeros_like(side_cols))
    top_row = jnp.where(tile_at == 0, row_lines[0], upper_row)
    bottom_row = jnp.where(tile_at == tile_count - 1, row_lines[1], lower_row)
    middle = jnp.concatenate([top_row[:, None, :], latent, bottom_row[:, None, :]], axis=1)
    padded = jnp.concatenate([side_cols[0][:, :, None], middle, side_cols[1][:, :, None]], axis=2)
    scale = 1.0 / math.sqrt(face_count * line_len * line_len)
    output, grad_one, grad_two, grad_kernel = strip_work(
        padded, latent, cotangent[0], kernel, ln_gain, ln_bias, w_one, b_one, w_two, b_two, scale
    )
    grad_one, grad_two, grad_kernel = lax.psum((grad_one, grad_two, grad_kernel), ("face", "tile"))
    return (output[None], grad_one, grad_two, grad_kernel)


def solution(mesh):
    placed = (
        P(("face", "tile"), None, None),
        P(("face", "tile")),
        P(("face", "tile")),
        P(("face", "tile"), None, None),
        P(("face", "tile")),
        P(),
        P(),
        P(),
        P(),
        P(),
        P(),
        P(),
        P(),
        P(),
        P(),
        P("face", None, "tile", None),
    )
    return jax.shard_map(
        per_device,
        mesh=mesh,
        in_specs=placed,
        out_specs=(P("face", None, "tile", None), P(), P(), P()),
        check_vma=False,
    )
```

profile of v0, /device:TPU:1, one launch (start us, length us, event | category | flops | bytes accessed | tf_op | source)
XLA Modules:
  0.0 591.9 jit_solution(9418654939937501962)
XLA Ops:
  8.4 6.4 %scatter_fusion = s32[128,2]{0,1:T(2,128)S(1)} fusion(s32[128,2]{0,1:T(2,128)S(1)} %broadcast_in_dim.44, s32[128]{0:T(128)S(1)} %fusion.33, s32[128]{0:T(128)S(1)} %get-tuple-element.43), kind=kCustom, calls=%fused_computation.3 | custom fusion | bytes 2560 | tf_op jit(solution)/shard_map/scatter | solution.py:152
  15.5 11.5 %all-to-all-start.1 = ((s32[128,1,2]{2,1,0:T(1,128)}), s32[128,1,2]{2,1,0:T(1,128)S(1)}, u32[]{:S(2)}, u32[]{:S(2)}) async-start(s32[128,1,2]{2,1,0:T(1,128)} %copy.79), calls=%async_computation.1 | async-start | bytes 131072 | tf_op jit(solution)/shard_map/all_to_all | solution.py:156
  28.4 3.4 convolution_convert_fusion
  31.8 1.1 broadcast_in_dim.46
  33.0 13.3 %scatter_fusion.1 = bf16[128,2,16,128]{3,2,1,0:T(8,128)(2,1)} fusion(bf16[128,2,16,128]{3,2,1,0:T(8,128)(2,1)} %broadcast_in_dim.46, s32[128]{0:T(128)S(1)} %fusion.33, bf16[128,16,128]{2,1,0:T(8,128)(2,1)S(1)} %convolution_convert_fusion), kind=kCustom, calls=%fused_computation.4 | custom fusion | bytes 1573888 | tf_op jit(solution)/shard_map/scatter | solution.py:149
  46.2 9.8 %all-to-all-start.2 = ((bf16[128,2,16,128]{3,2,1,0:T(8,128)(2,1)}), bf16[128,2,16,128]{3,2,1,0:T(8,128)(2,1)S(1)}, u32[]{:S(2)}, u32[]{:S(2)}) async-start(bf16[128,2,16,128]{3,2,1,0:T(8,128)(2,1)} %scatter_fusion.1), calls=%async_computation.2 | async-start | bytes 2097152 | tf_op jit(solution)/shard_map/all_to_all | solution.py:155
  59.2 15.7 %all-to-all-done.2 = bf16[128,2,16,128]{3,2,1,0:T(8,128)(2,1)S(1)} async-done(((bf16[128,2,16,128]{3,2,1,0:T(8,128)(2,1)}), bf16[128,2,16,128]{3,2,1,0:T(8,128)(2,1)S(1)}, u32[]{:S(2)}, u32[]{:S(2)}) %all-to-all-start.2) | async-done | bytes 1048608 | tf_op jit(solution)/shard_map/all_to_all | solution.py:155
  74.9 4.5 all-to-all-start
  79.8 9.2 %scatter_fusion.2 = f32[128,16,128]{2,1,0:T(8,128)S(1)} fusion(f32[128,16,128]{2,1,0:T(8,128)S(1)} %broadcast_in_dim.43, s32[256]{0:T(256)S(1)} %bitcast.183, f32[256,16,128]{2,1,0:T(8,128)S(1)} %bitcast_convert_fusion), kind=kCustom, calls=%fused_computation.5 | custom fusion | flops 524288 | bytes 6292480 | tf_op jit(solution)/shard_map/scatter-add | solution.py:159
  90.0 13.2 %scatter_fusion.3 = bf16[128,16,128]{2,1,0:T(8,128)(2,1)} fusion(bf16[128,16,128]{2,1,0:T(8,128)(2,1)} %broadcast.194.clone, s32[128]{0:T(128)S(1)} %get-tuple-element.46, bf16[128,16,128]{2,1,0:T(8,128)(2,1)S(1)} %convert_element_type.45), kind=kCustom, calls=%fused_computation.6 | custom fusion | bytes 1573376 | tf_op jit(solution)/shard_map/scatter | solution.py:165
  103.1 9.8 %all-to-all-start.3 = ((bf16[128,16,128]{2,1,0:T(8,128)(2,1)}), bf16[128,16,128]{2,1,0:T(8,128)(2,1)S(1)}, u32[]{:S(2)}, u32[]{:S(2)}) async-start(bf16[128,16,128]{2,1,0:T(8,128)(2,1)} %scatter_fusion.3), calls=%async_computation.3 | async-start | bytes 1048576 | tf_op jit(solution)/shard_map/all_to_all | solution.py:168
  113.5 2.4 reduce.4
  115.8 10.7 %all-to-all-done.3 = bf16[128,16,128]{2,1,0:T(8,128)(2,1)S(1)} async-done(((bf16[128,16,128]{2,1,0:T(8,128)(2,1)}), bf16[128,16,128]{2,1,0:T(8,128)(2,1)S(1)}, u32[]{:S(2)}, u32[]{:S(2)}) %all-to-all-start.3) | async-done | bytes 524320 | tf_op jit(solution)/shard_map/all_to_all | solution.py:168
  127.4 13.2 %scatter_fusion.4 = bf16[128,16,128]{2,1,0:T(8,128)(2,1)} fusion(bf16[128,16,128]{2,1,0:T(8,128)(2,1)} %broadcast.194, s32[128]{0:T(128)S(1)} %fusion.31, bf16[128,16,128]{2,1,0:T(8,128)(2,1)S(1)} %all-to-all-done.3), kind=kCustom, calls=%fused_computation.7 | custom fusion | bytes 1573376 | tf_op jit(solution)/shard_map/scatter | solution.py:171
  140.6 2.0 fusion.7
  142.6 1.2 copy.102
  143.9 1.7 copy-done.3
  147.3 2.7 fusion.40
  150.0 1.9 copy.100
  151.9 1.9 copy.99
  154.1 23.3 %all-gather = bf16[16,1,5760]{2,1,0:T(2,128)(2,1)} all-gather(bf16[1,1,5760]{2,1,0:T(2,128)(2,1)S(1)} %reshape.282), channel_id=1, replica_groups=mesh['face'=8,'tile'=16] {'tile'}, dimensions={0}, use_global_device_ids=true | all-gather | bytes 195840 | tf_op jit(solution)/shard_map/all_gather | solution.py:180
  177.4 2.0 reduce.6
  179.4 1.8 reshape.215
  181.2 2.1 slice_bitcast_fusion.2
  183.2 1.2 copy.87
  184.6 1.2 copy.86
  185.9 4.6 all-gather.4.cloned.1.call-done
  190.5 1.6 fusion.41
  193.0 1.6 slice.143
  194.6 1.7 pad_maximum_fusion
  196.3 2.0 reshape.216
  198.7 2.3 pad.18
  201.0 3.7 copy.107
  205.1 3.8 slice.204
  209.0 3.1 collective-permute-start
  212.0 1.9 collective-permute-start.1
  214.0 24.0 %all-gather.6.cloned.1.call-done = bf16[1474560]{0:T(1024)(128)(2,1)} async-done(((bf16[184320]{0:T(1024)(128)(2,1)}), bf16[1474560]{0:T(1024)(128)(2,1)}) %all-gather.6.cloned.1.call-update) | async-done | bytes 2949136 | tf_op jit(solution)/shard_map/all_gather | solution.py:186
  238.0 5.6 reshape.217
  243.6 3.2 gather_fusion.1
  246.8 8.5 %rev.3 = bf16[4,90,512]{2,1,0:T(8,128)(2,1)} reverse(bf16[4,90,512]{2,1,0:T(8,128)(2,1)} %gather_fusion.1), dimensions={2} | reverse | bytes 737280 | tf_op jit(solution)/shard_map/rev | solution.py:191
  255.3 1.2 broadcast_select_fusion
  257.5 1.6 copy.94
  259.1 1.0 fusion.20
  261.1 1.6 copy.93
  262.7 8.9 %maximum_convert_fusion = f32[90,34,514]{2,1,0:T(8,128)} fusion(bf16[90,34,1]{2,1,0:T(8,128)(2,1)} %copy.94, bf16[90,1,512]{2,1,0:T(2,128)(2,1)S(1)} %copy.91, bf16[90,32,512]{2,1,0:T(8,128)(2,1)} %slice.204, bf16[90,1,512]{2,1,0:T(2,128)(2,1)} %copy.90, bf16[90,34,1]{2,1,0:T(8,128)(2,1)} %copy.93), kind=kLoop, calls=%fused_computation.45 | loop fusion | flops 15728400 | bytes 9437040 | tf_op jit(solution)/shard_map/convert_element_type | solution.py:50
  271.6 34.9 %fusion.38 = (f32[32,512]{1,0:T(8,128)S(1)}, f32[90,32,512]{2,1,0:T(8,128)}) fusion(f32[90,34,514]{2,1,0:T(8,128)} %maximum_convert_fusion, f32[90]{0:T(128)S(1)} %get-tuple-element.41, f32[90]{0:T(128)S(1)} %get-tuple-element.42, f32[90]{0:T(128)S(1)} %get-tuple-element.35, f32[90]{0:T(128)S(1)} %get-tuple-element.36, f32[90]{0:T(128)S(1)} %get-tuple-element.37, ...), kind=kLoop, calls=%fused_computation.128 | loop fusion | flops 26525696 | bytes 59051176 | tf_op jit(solution)/shard_map/reduce_sum | solution.py:58
  306.5 3.5 pad.17
  310.1 4.3 copy.103
  315.5 15.2 %multiply_convert_fusion = (bf16[360,16384]{1,0:T(8,128)(2,1)}, f32[16384,360]{0,1:T(8,128)}) fusion(f32[360]{0:T(512)S(1)} %copy-done.16, bf16[90,360]{1,0:T(8,128)(2,1)S(1)} %copy-done.7, f32[90,16384]{1,0:T(8,128)S(1)} %bitcast.150, f32[90]{0:T(128)S(1)} %copy-done.15, f32[90]{0:T(128)S(1)} %copy-done.10, f32[16384]{0:T(1024)S(1)} %bitcast.169, ...), kind=kOutput, calls=%fused_computation.18 | convolution fusion | flops 1128038400 | bytes 41485712 | tf_op jit(solution)/shard_map/dot_general | solution.py:64
  330.7 20.6 %fusion.6 = bf16[360,16384]{1,0:T(8,128)(2,1)} fusion(f32[16384,360]{0,1:T(8,128)} %get-tuple-element.48, bf16[360,90]{0,1:T(8,128)(2,1)S(1)} %copy-done.8, bf16[90,16384]{1,0:T(8,128)(2,1)S(1)} %bitcast.165), kind=kOutput, calls=%fused_computation.16 | convolution fusion | flops 1173749760 | bytes 38403360 | tf_op jit(solution)/shard_map/dot_general | solution.py:75
  351.3 8.7 %convolution_multiply_fusion.1 = f32[90,360]{1,0:T(8,128)} fusion(bf16[360,16384]{1,0:T(8,128)(2,1)} %fusion.6, f32[90,16384]{1,0:T(8,128)S(1)} %bitcast.151, f32[90]{0:T(128)S(1)} %copy-done.15, f32[90]{0:T(128)S(1)} %copy-done.10, f32[16384]{0:T(1024)S(1)} %bitcast.170, f32[16384]{0:T(1024)S(1)} %bitcast.174), kind=kOutput, calls=%fused_computation.48 | convolution fusion | flops 1069088384 | bytes 17956112 | tf_op jit(solution)/shard_map/dot_general | solution.py:41
  360.0 10.5 %fusion.13 = (f32[16384]{0:T(1024)S(1)}, f32[16384,90]{0,1:T(8,128)}) fusion(f32[90,16384]{1,0:T(8,128)S(1)} %bitcast.152, f32[16384]{0:T(1024)S(1)} %bitcast.171, f32[16384]{0:T(1024)S(1)} %bitcast.175, f32[90]{0:T(128)S(1)} %copy-done.10, bf16[360,16384]{1,0:T(8,128)(2,1)} %fusion.6, bf16[90,360]{1,0:T(8,128)(2,1)S(1)} %copy-done.7), kind=kOutput, calls=%fused_computation.31 | convolution fusion | flops 1069039616 | bytes 23854728 | tf_op jit(solution)/shard_map/dot_general | solution.py:78
  370.6 8.6 %convolution_multiply_fusion.2 = f32[360,90]{0,1:T(8,128)} fusion(bf16[360,16384]{1,0:T(8,128)(2,1)} %get-tuple-element.47, bf16[90,16384]{1,0:T(8,128)(2,1)S(1)} %bitcast.166), kind=kOutput, calls=%fused_computation.49 | convolution fusion | flops 1061715584 | bytes 14875200 | tf_op jit(solution)/shard_map/dot_general | solution.py:41
  379.1 6.9 %fusion.10 = bf16[90,16384]{1,0:T(8,128)(2,1)S(1)} fusion(bf16[360,16384]{1,0:T(8,128)(2,1)} %get-tuple-element.47, bf16[360,90]{0,1:T(8,128)(2,1)S(1)} %copy-done.8, bf16[16384,90]{0,1:T(8,128)(2,1)S(1)} %fusion.7, f32[90]{0:T(128)S(1)} %copy-done.11), kind=kOutput, calls=%fused_computation.26 | convolution fusion | flops 1067581440 | bytes 17759880 | tf_op jit(solution)/shard_map/dot_general | solution.py:68
  386.0 1.5 copy.106
  387.5 2.0 slice_bitcast_fusion
  389.5 3.2 reduce_sum.132
  392.7 6.2 %fusion.12 = f32[90,16384]{1,0:T(8,128)S(1)} fusion(f32[16384,90]{0,1:T(8,128)} %get-tuple-element.50, f32[90,16384]{1,0:T(8,128)} %bitcast.153, f32[16384]{0:T(1024)S(1)} %broadcast_multiply_fusion, f32[16384]{0:T(1024)S(1)} %broadcast_multiply_fusion.1, f32[16384]{0:T(1024)S(1)} %bitcast.172, f32[16384]{0:T(1024)S(1)} %bitcast.176), kind=kLoop, calls=%fused_computation.30 | loop fusion | flops 8847360 | bytes 17956864 | tf_op jit(solution)/shard_map/mul | solution.py:79
  398.9 7.0 %copy.108 = f32[12,8,32,512]{3,2,1,0:T(8,128)} copy(f32[12,8,32,512]{3,1,2,0:T(8,128)S(1)} %bitcast.158) | data formatting | bytes 12582912
  405.9 31.9 %multiply_reduce_fusion = (f32[90]{0:T(128)S(1)}, f32[90]{0:T(128)S(1)}, f32[90]{0:T(128)S(1)}, f32[90]{0:T(128)S(1)}, f32[90]{0:T(128)S(1)}, /*index=5*/f32[90]...) fusion(f32[90,34,514]{2,1,0:T(8,128)} %maximum_convert_fusion, f32[96,32,512]{2,1,0:T(8,128)} %bitcast.159), kind=kLoop, calls=%fused_computation.34 | loop fusion | flops 26541270 | bytes 58985640 | tf_op jit(solution)/shard_map/reduce_sum | solution.py:90
  437.8 67.0 %psum.23 = f32[9,90]{1,0:T(8,128)} all-reduce(f32[9,90]{1,0:T(8,128)S(1)} %broadcast_multiply_fusion.3), channel_id=1, replica_groups=mesh['face'=8,'tile'=16] {'face','tile'}, use_global_device_ids=true, to_apply=%region_23.24 | all-reduce | flops 810 | bytes 6480 | tf_op jit(solution)/shard_map/psum | solution.py:210
  504.8 77.2 %all-reduce.4.cloned.1.call-done = (f32[90,360]{1,0:T(8,128)}, f32[360,90]{0,1:T(8,128)}) async-done(((f32[90,360]{1,0:T(8,128)}, f32[360,90]{0,1:T(8,128)}), (f32[90,360]{1,0:T(8,128)}, f32[360,90]{0,1:T(8,128)})) %all-reduce.4.cloned.1.call-update) | async-done | bytes 259216 | tf_op jit(solution)/shard_map/psum | solution.py:210
  582.0 1.6 copy.123
  583.5 1.6 copy.124
  (102 shorter events, 16.0 us)
Async XLA Ops:
  7.2 20.5 %copy-start = (bf16[64,16,128]{2,1,0:T(8,128)(2,1)S(1)}, bf16[64,16,128]{2,1,0:T(8,128)(2,1)}, u32[]{:S(2)}) copy-start(bf16[64,16,128]{2,1,0:T(8,128)(2,1)} %param.16) | copy-start | bytes 786436
  8.0 48.0 %copy-start.17 = (s32[128]{0:T(128)S(1)}, s32[128]{0:T(128)}, u32[]{:S(2)}) copy-start(s32[128]{0:T(128)} %param.20) | copy-start | bytes 1540
  15.5 30.7 %all-to-all-start.1 = ((s32[128,1,2]{2,1,0:T(1,128)}), s32[128,1,2]{2,1,0:T(1,128)S(1)}, u32[]{:S(2)}, u32[]{:S(2)}) async-start(s32[128,1,2]{2,1,0:T(1,128)} %copy.79), calls=%async_computation.1 | async-start | bytes 131072 | tf_op jit(solution)/shard_map/all_to_all | solution.py:156
  46.2 28.7 %all-to-all-start.2 = ((bf16[128,2,16,128]{3,2,1,0:T(8,128)(2,1)}), bf16[128,2,16,128]{3,2,1,0:T(8,128)(2,1)S(1)}, u32[]{:S(2)}, u32[]{:S(2)}) async-start(bf16[128,2,16,128]{3,2,1,0:T(8,128)(2,1)} %scatter_fusion.1), calls=%async_computation.2 | async-start | bytes 2097152 | tf_op jit(solution)/shard_map/all_to_all | solution.py:155
  74.9 28.2 %all-to-all-start = ((s32[128,1,1]{2,1,0:T(1,128)}), s32[128,1,1]{2,1,0:T(1,128)S(1)}, u32[]{:S(2)}, u32[]{:S(2)}) async-start(s32[128,1,1]{2,1,0:T(1,128)} %copy.78), calls=%async_computation | async-start | bytes 131072 | tf_op jit(solution)/shard_map/all_to_all | solution.py:169
  79.8 60.8 %copy-start.12 = (bf16[16,90]{1,0:T(8,128)(2,1)S(1)}, bf16[16,90]{1,0:T(8,128)(2,1)}, u32[]{:S(2)}) copy-start(bf16[16,90]{1,0:T(8,128)(2,1)} %param.22) | copy-start | bytes 8644
  79.8 60.8 %copy-start.14 = (f32[90]{0:T(128)S(1)}, f32[90]{0:T(128)}, u32[]{:S(2)}) copy-start(f32[90]{0:T(128)} %param.23) | copy-start | bytes 1084
  103.1 23.4 %all-to-all-start.3 = ((bf16[128,16,128]{2,1,0:T(8,128)(2,1)}), bf16[128,16,128]{2,1,0:T(8,128)(2,1)S(1)}, u32[]{:S(2)}, u32[]{:S(2)}) async-start(bf16[128,16,128]{2,1,0:T(8,128)(2,1)} %scatter_fusion.3), calls=%async_computation.3 | async-start | bytes 1048576 | tf_op jit(solution)/shard_map/all_to_all | solution.py:168
  113.0 77.5 %all-gather.4.cloned.1.call-start = ((), (), s32[]{:S(2)}) async-start(), calls=%async_computation.4 | async-start | bytes 1566720 | tf_op jit(solution)/shard_map/all_gather | solution.py:179
  143.9 1.7 copy-start.3
  146.5 52.0 %copy-start.9 = (s32[8,4,3]{0,1,2:T(4,128)S(1)}, s32[8,4,3]{0,1,2:T(4,128)}, u32[]{:S(2)}) copy-start(s32[8,4,3]{0,1,2:T(4,128)} %param.21) | copy-start | bytes 1156
  147.3 90.7 %all-gather.6.cloned.1.call-start = ((), (), s32[]{:S(2)}) async-start(), calls=%async_computation.5 | async-start | bytes 3317760 | tf_op jit(solution)/shard_map/all_gather | solution.py:186
  198.3 6.8 %copy-start.13 = (f32[9,90]{1,0:T(8,128)S(1)}, f32[9,90]{1,0:T(8,128)}, u32[]{:S(2)}) copy-start(f32[9,90]{1,0:T(8,128)} %param.24) | copy-start | bytes 9724
  198.3 383.7 %all-reduce.4.cloned.1.call-start = ((), (), s32[]{:S(2)}) async-start(), calls=%async_computation.6 | async-start | bytes 589824 | tf_op jit(solution)/shard_map/psum | solution.py:210
  209.0 50.1 %collective-permute-start = (bf16[90,1,512]{2,0,1:T(8,128)(2,1)}, bf16[90,1,512]{2,0,1:T(8,128)(2,1)S(1)}, u32[]{:S(2)}, u32[]{:S(2)}) collective-permute-start(bf16[90,1,512]{2,0,1:T(8,128)(2,1)} %get-tuple-element.18), channel_id=1, source_target_pairs={{0,1},{1,2},{2,3},{3,4},{4,5},{5,6},{6,7},{7,8},{8,9},{9,10},{10,1... | collective-permute-start | bytes 276488 | tf_op jit(solution)/shard_map/ppermute | solution.py:21
  212.0 47.1 %collective-permute-start.1 = (bf16[90,1,512]{2,0,1:T(8,128)(2,1)}, bf16[90,1,512]{2,0,1:T(8,128)(2,1)}, u32[]{:S(2)}, u32[]{:S(2)}) collective-permute-start(bf16[90,1,512]{2,0,1:T(8,128)(2,1)} %get-tuple-element.19), channel_id=1, source_target_pairs={{1,0},{2,1},{3,2},{4,3},{5,4},{6,5},{7,6},{8,7},{9,8},{10,9},{11,1... | collective-permute-start | bytes 276488 | tf_op jit(solution)/shard_map/ppermute | solution.py:23
  256.5 0.8 copy-start.6
  306.5 8.0 %slice-start = ((s8[5898240]{0:T(1024)(128)(4,1)}), s8[4194304]{0:T(1024)(128)(4,1)S(1)}, s32[]{:S(2)}) async-start(s8[5898240]{0:T(1024)(128)(4,1)} %bitcast.154), calls=%async_computation.7 | async-start | bytes 8388608
  310.1 4.5 slice-start.1
  314.5 45.5 %copy-start.2 = (f32[12,8,32,512]{3,1,2,0:T(8,128)}, f32[12,8,32,512]{3,1,2,0:T(8,128)S(1)}, u32[]{:S(2)}) copy-start(f32[12,8,32,512]{3,1,2,0:T(8,128)S(1)} %copy.103) | copy-start | bytes 18874372
  314.5 1.0 copy-start.7
  314.5 0.9 copy-start.10
  314.5 0.9 copy-start.15
  314.5 0.9 copy-start.16
  315.4 15.2 %copy-start.4 = (bf16[12,8,32,512]{3,1,2,0:T(8,128)(2,1)S(1)}, bf16[12,8,32,512]{3,1,2,0:T(8,128)(2,1)}, u32[]{:S(2)}) copy-start(bf16[12,8,32,512]{3,1,2,0:T(8,128)(2,1)} %copy.107) | copy-start | bytes 9437188
  315.4 15.2 %copy-start.8 = (bf16[360,90]{0,1:T(8,128)(2,1)S(1)}, bf16[360,90]{0,1:T(8,128)(2,1)}, u32[]{:S(2)}) copy-start(bf16[360,90]{0,1:T(8,128)(2,1)} %param.29) | copy-start | bytes 194404
  360.0 10.6 %copy-start.5 = (bf16[12,8,32,512]{3,1,2,0:T(8,128)(2,1)S(1)}, bf16[12,8,32,512]{3,1,2,0:T(8,128)(2,1)}, u32[]{:S(2)}) copy-start(bf16[12,8,32,512]{3,1,2,0:T(8,128)(2,1)} %copy.107) | copy-start | bytes 9437188
  370.6 8.6 %copy-start.11 = (f32[90]{0:T(128)S(1)}, f32[90]{0:T(128)}, u32[]{:S(2)}) copy-start(f32[90]{0:T(128)} %param.30) | copy-start | bytes 1084
  405.9 179.2 %copy-start.1 = (bf16[64,16,128]{2,1,0:T(8,128)(2,1)S(1)}, bf16[64,16,128]{2,1,0:T(8,128)(2,1)}, u32[]{:S(2)}) copy-start(bf16[64,16,128]{2,1,0:T(8,128)(2,1)} %param.16) | copy-start | bytes 786436
Sparse Core Ops, SparseCore 0:
  147.4 43.0 all-gather.3
  198.4 39.5 all-gather.5
  437.9 144.0 all-reduce.3
where the time goes:
time: 601 us; the launch traced here: 592 us
  waiting for transfers between devices  132 us (22%)
  local copies, waits for them, and re-layouts  130 us (22%)
  other arithmetic  107 us (18%)
  blocking collectives  90.3 us (15%)
  matrix products  76 us (13%)
  starting transfers between devices  41.3 us (7%)
  between operations  14.6 us (2%)
    psum x1, waiting for transfers between devices, per_device(): lax.psum((grad_one, grad_two, grad_kernel), ('face', 'tile'))  77.2 us
    psum x1, blocking collectives, per_device(): lax.psum((grad_one, grad_two, grad_kernel), ('face', 'tile'))  67 us
    reduce_sum x1, other arithmetic, strip_work(): mean_val = jnp.mean(flat, axis=0, keepdims=True)  34.9 us
    unnamed x54, local copies, waits for them, and re-layouts  33.3 us
    reduce_sum x1, other arithmetic, strip_work(): kernel_rows.append(jnp.sum(back_grid * window, axis=(1, 2)))  31.9 us
    all_gather x1, waiting for transfers between devices, per_device(): lax.all_gather(own_lines.reshape(-1), 'face', axis=0, tiled=True)  24 us
    all_gather x1, blocking collectives, per_device(): lax.all_gather(edge_cols.reshape(-1), 'tile', axis=0, tiled=True)  23.3 us
    dot_general x1, matrix products, strip_work(): back_hidden = jnp.dot(w_two, cot_flat, preferred_element_type=jnp.float32)  20.6 us
  transfers between devices with their start and end apart: 9, of which 5 were waited for; matrix products, arithmetic and copies ran while one was open for 16% of the time, Pallas kernels for 0%

commit v1 on v0

--- a/solution.py
+++ b/solution.py
@@ -183,9 +183,10 @@
         rows_face.reshape(tile_count, chan_count, line_len),
         cols_face.reshape(tile_count, 2, chan_count, row_count),
     )
-    all_lines = lax.all_gather(own_lines.reshape(-1), "face", axis=0, tiled=True).reshape(
-        face_count, 4, chan_count, line_len
-    )
+    all_lines = jnp.concatenate(
+        lax.all_to_all(jnp.stack([own_lines.reshape(-1)] * lax.axis_size("face")), "face", 0, 0),
+        axis=0,
+    ).reshape(face_count, 4, chan_count, line_len)
     face_link = face_links[face_at]
     picked = all_lines[face_link[:, 0], face_link[:, 1]]
     picked = jnp.where(face_link[:, 2][:, None, None] == 1, picked[:, :, ::-1], picked)

time: 601 us -> 684 us (1.14)
  other arithmetic: 107 us -> 162 us
  local copies, waits for them, and re-layouts: 130 us -> 152 us
    another operation x0 -> x1, other arithmetic: none -> 54.4 us  [per_device(): jnp.stack([own_lines.reshape(-1)] * lax.axis_size('face'))]
    all_gather x1 -> x0, waiting for transfers between devices: 24 us -> none  [per_device(): lax.all_gather(own_lines.reshape(-1), 'face', axis=0, tiled=True)]
    all_to_all x0 -> x1, waiting for transfers between devices: none -> 20.4 us  [per_device(): lax.all_to_all(jnp.stack([own_lines.reshape(-1)] * lax.axis_size('face'))...]
    unnamed x54 -> x56, local copies, waits for them, and re-layouts: 33.3 us -> 47.2 us
    another operation x2 -> x6, local copies, waits for them, and re-layouts: 1.73 us -> 12.7 us  [the longest x3 8.25 us: per_device(): jnp.stack([own_lines.reshape(-1)] * lax.axis_size('face'))]
    reshape x2 -> x0, local copies, waits for them, and re-layouts: 7.6 us -> none  [the longest x1 5.65 us: per_device(): lax.all_gather(own_lines.reshape(-1), 'face', axis=0, tiled=True)]
  transfers between devices with their start and end apart: 9 -> 9, of which waited for: 5 -> 5; matrix products, arithmetic and copies ran while one was open for 16% -> 15% of each run, Pallas kernels for 0% -> 0%
where the time goes in v1:
time: 684 us; the launch traced here: 675 us
  other arithmetic  162 us (24%)
  local copies, waits for them, and re-layouts  152 us (22%)
  waiting for transfers between devices  128 us (19%)
  blocking collectives  96.1 us (14%)
  matrix products  76.1 us (11%)
  starting transfers between devices  45.6 us (7%)
  between operations  14.8 us (2%)
    psum x1, waiting for transfers between devices, per_device(): lax.psum((grad_one, grad_two, grad_kernel), ('face', 'tile'))  76.5 us
    psum x1, blocking collectives, per_device(): lax.psum((grad_one, grad_two, grad_kernel), ('face', 'tile'))  72.7 us
    another operation x1, other arithmetic, per_device(): jnp.stack([own_lines.reshape(-1)] * lax.axis_size('face'))  54.4 us
    unnamed x56, local copies, waits for them, and re-layouts  47.2 us
    reduce_sum x1, other arithmetic, strip_work(): mean_val = jnp.mean(flat, axis=0, keepdims=True)  34.7 us
    reduce_sum x1, other arithmetic, strip_work(): kernel_rows.append(jnp.sum(back_grid * window, axis=(1, 2)))  31.8 us
    all_gather x1, blocking collectives, per_device(): lax.all_gather(edge_cols.reshape(-1), 'tile', axis=0, tiled=True)  23.4 us
    dot_general x1, matrix products, strip_work(): back_hidden = jnp.dot(w_two, cot_flat, preferred_element_type=jnp.float32)  20.6 us
  transfers between devices with their start and end apart: 9, of which 5 were waited for; matrix products, arithmetic and copies ran while one was open for 15% of the time, Pallas kernels for 0%

profile of v1, /device:TPU:1, one launch (start us, length us, event | category | flops | bytes accessed | tf_op | source)
XLA Modules:
  0.0 674.7 jit_solution(9910259348530299273)
XLA Ops:
  8.4 6.4 scatter_fusion
  15.5 11.5 %all-to-all-start.1 = ((s32[128,1,2]{2,1,0:T(1,128)}), s32[128,1,2]{2,1,0:T(1,128)S(1)}, u32[]{:S(2)}, u32[]{:S(2)}) async-start(s32[128,1,2]{2,1,0:T(1,128)} %copy.85), calls=%async_computation.1 | async-start | bytes 131072 | tf_op jit(solution)/shard_map/all_to_all | solution.py:156
  28.4 3.4 convolution_convert_fusion
  33.0 13.3 %scatter_fusion.1 = bf16[128,2,16,128]{3,2,1,0:T(8,128)(2,1)} fusion(bf16[128,2,16,128]{3,2,1,0:T(8,128)(2,1)} %broadcast_in_dim.46, s32[128]{0:T(128)S(1)} %fusion.33, bf16[128,16,128]{2,1,0:T(8,128)(2,1)S(1)} %convolution_convert_fusion), kind=kCustom, calls=%fused_computation.4 | custom fusion | bytes 1573888 | tf_op jit(solution)/shard_map/scatter | solution.py:149
  46.2 9.8 %all-to-all-start.2 = ((bf16[128,2,16,128]{3,2,1,0:T(8,128)(2,1)}), bf16[128,2,16,128]{3,2,1,0:T(8,128)(2,1)S(1)}, u32[]{:S(2)}, u32[]{:S(2)}) async-start(bf16[128,2,16,128]{3,2,1,0:T(8,128)(2,1)} %scatter_fusion.1), calls=%async_computation.2 | async-start | bytes 2097152 | tf_op jit(solution)/shard_map/all_to_all | solution.py:155
  59.2 15.7 %all-to-all-done.2 = bf16[128,2,16,128]{3,2,1,0:T(8,128)(2,1)S(1)} async-done(((bf16[128,2,16,128]{3,2,1,0:T(8,128)(2,1)}), bf16[128,2,16,128]{3,2,1,0:T(8,128)(2,1)S(1)}, u32[]{:S(2)}, u32[]{:S(2)}) %all-to-all-start.2) | async-done | bytes 1048608 | tf_op jit(solution)/shard_map/all_to_all | solution.py:155
  74.9 4.5 all-to-all-start
  79.8 9.2 %scatter_fusion.2 = f32[128,16,128]{2,1,0:T(8,128)S(1)} fusion(f32[128,16,128]{2,1,0:T(8,128)S(1)} %broadcast_in_dim.43, s32[256]{0:T(256)S(1)} %bitcast.185, f32[256,16,128]{2,1,0:T(8,128)S(1)} %bitcast_convert_fusion), kind=kCustom, calls=%fused_computation.5 | custom fusion | flops 524288 | bytes 6292480 | tf_op jit(solution)/shard_map/scatter-add | solution.py:159
  90.0 13.2 %scatter_fusion.3 = bf16[128,16,128]{2,1,0:T(8,128)(2,1)} fusion(bf16[128,16,128]{2,1,0:T(8,128)(2,1)} %broadcast.198.clone, s32[128]{0:T(128)S(1)} %get-tuple-element.46, bf16[128,16,128]{2,1,0:T(8,128)(2,1)S(1)} %convert_element_type.45), kind=kCustom, calls=%fused_computation.6 | custom fusion | bytes 1573376 | tf_op jit(solution)/shard_map/scatter | solution.py:165
  103.1 9.8 %all-to-all-start.3 = ((bf16[128,16,128]{2,1,0:T(8,128)(2,1)}), bf16[128,16,128]{2,1,0:T(8,128)(2,1)S(1)}, u32[]{:S(2)}, u32[]{:S(2)}) async-start(bf16[128,16,128]{2,1,0:T(8,128)(2,1)} %scatter_fusion.3), calls=%async_computation.3 | async-start | bytes 1048576 | tf_op jit(solution)/shard_map/all_to_all | solution.py:168
  113.2 2.4 reduce.4
  115.6 11.0 %all-to-all-done.3 = bf16[128,16,128]{2,1,0:T(8,128)(2,1)S(1)} async-done(((bf16[128,16,128]{2,1,0:T(8,128)(2,1)}), bf16[128,16,128]{2,1,0:T(8,128)(2,1)S(1)}, u32[]{:S(2)}, u32[]{:S(2)}) %all-to-all-start.3) | async-done | bytes 524320 | tf_op jit(solution)/shard_map/all_to_all | solution.py:168
  127.4 13.2 %scatter_fusion.4 = bf16[128,16,128]{2,1,0:T(8,128)(2,1)} fusion(bf16[128,16,128]{2,1,0:T(8,128)(2,1)} %broadcast.198, s32[128]{0:T(128)S(1)} %fusion.31, bf16[128,16,128]{2,1,0:T(8,128)(2,1)S(1)} %all-to-all-done.3), kind=kCustom, calls=%fused_computation.7 | custom fusion | bytes 1573376 | tf_op jit(solution)/shard_map/scatter | solution.py:171
  140.6 2.0 fusion.7
  143.9 1.7 copy-done.3
  147.3 2.8 fusion.40
  150.1 1.9 copy.111
  152.0 1.9 copy.110
  154.1 23.4 %all-gather = bf16[16,1,5760]{2,1,0:T(2,128)(2,1)} all-gather(bf16[1,1,5760]{2,1,0:T(2,128)(2,1)S(1)} %reshape.284), channel_id=1, replica_groups=mesh['face'=8,'tile'=16] {'tile'}, dimensions={0}, use_global_device_ids=true | all-gather | bytes 195840 | tf_op jit(solution)/shard_map/all_gather | solution.py:180
  177.5 2.0 reduce.6
  179.5 1.8 reshape.219
  181.3 2.1 slice_bitcast_fusion.2
  186.1 4.5 all-gather.3.cloned.1.call-done
  190.6 1.6 fusion.41
  193.1 1.6 slice.143
  194.7 1.7 pad_maximum_fusion
  196.4 2.0 stack.43
  198.4 5.7 stack.44
  204.6 54.4 %reduce.13 = bf16[8,184320]{1,0:T(8,128)(2,1)} reduce(bf16[8,1,184320]{2,1,0:T(2,128)(2,1)} %stack.44, bf16[]{:T(256)} %broadcast.331), dimensions={1}, to_apply=%stack.44.reduce_sub_computation | reduce | bytes 5898242 | tf_op jit(solution)/shard_map/stack | solution.py:187
  259.0 6.1 reshape.303
  265.1 4.5 all-to-all-start.4
  269.9 2.3 pad.18
  272.1 3.7 copy.118
  276.3 3.8 slice.204
  280.1 2.9 collective-permute-start
  283.1 2.4 collective-permute-start.1
  285.5 20.4 %all-to-all-done.4 = bf16[8,2,92160]{2,1,0:T(2,128)(2,1)} async-done(((bf16[8,2,92160]{2,1,0:T(2,128)(2,1)}), bf16[8,2,92160]{2,1,0:T(2,128)(2,1)}, u32[]{:S(2)}, u32[]{:S(2)}) %all-to-all-start.4) | async-done | bytes 2949152 | tf_op jit(solution)/shard_map/all_to_all | solution.py:187
  305.9 7.6 %reshape.304 = bf16[8,1,184320]{2,1,0:T(2,128)(2,1)} reshape(bf16[8,2,92160]{2,1,0:T(2,128)(2,1)} %all-to-all-done.4) | data formatting | bytes 5898240
  313.5 4.9 copy.96
  318.4 2.7 copy.97
  321.1 3.2 gather_fusion.1
  324.3 8.5 %rev.3 = bf16[4,90,512]{2,1,0:T(8,128)(2,1)} reverse(bf16[4,90,512]{2,1,0:T(8,128)(2,1)} %gather_fusion.1), dimensions={2} | reverse | bytes 737280 | tf_op jit(solution)/shard_map/rev | solution.py:192
  334.9 1.6 copy.103
  338.6 1.6 copy.102
  340.2 8.9 %maximum_convert_fusion = f32[90,34,514]{2,1,0:T(8,128)} fusion(bf16[90,34,1]{2,1,0:T(8,128)(2,1)} %copy.103, bf16[90,1,512]{2,1,0:T(2,128)(2,1)S(1)} %copy.100, bf16[90,32,512]{2,1,0:T(8,128)(2,1)} %slice.204, bf16[90,1,512]{2,1,0:T(2,128)(2,1)} %copy.99, bf16[90,34,1]{2,1,0:T(8,128)(2,1)} %copy.102), kind=kLoop, calls=%fused_computation.45 | loop fusion | flops 15728400 | bytes 9437040 | tf_op jit(solution)/shard_map/convert_element_type | solution.py:50
  349.1 34.7 %fusion.38 = (f32[32,512]{1,0:T(8,128)S(1)}, f32[90,32,512]{2,1,0:T(8,128)}) fusion(f32[90,34,514]{2,1,0:T(8,128)} %maximum_convert_fusion, f32[90]{0:T(128)S(1)} %get-tuple-element.41, f32[90]{0:T(128)S(1)} %get-tuple-element.42, f32[90]{0:T(128)S(1)} %get-tuple-element.35, f32[90]{0:T(128)S(1)} %get-tuple-element.36, f32[90]{0:T(128)S(1)} %get-tuple-element.37, ...), kind=kLoop, calls=%fused_computation.128 | loop fusion | flops 26525696 | bytes 59051176 | tf_op jit(solution)/shard_map/reduce_sum | solution.py:58
  383.8 3.5 pad.17
  387.4 4.3 copy.114
  392.7 15.2 %multiply_convert_fusion = (bf16[360,16384]{1,0:T(8,128)(2,1)}, f32[16384,360]{0,1:T(8,128)}) fusion(f32[360]{0:T(512)S(1)} %copy-done.16, bf16[90,360]{1,0:T(8,128)(2,1)S(1)} %copy-done.7, f32[90,16384]{1,0:T(8,128)S(1)} %bitcast.151, f32[90]{0:T(128)S(1)} %copy-done.15, f32[90]{0:T(128)S(1)} %copy-done.10, f32[16384]{0:T(1024)S(1)} %bitcast.171, ...), kind=kOutput, calls=%fused_computation.18 | convolution fusion | flops 1128038400 | bytes 41485712 | tf_op jit(solution)/shard_map/dot_general | solution.py:64
  407.9 20.6 %fusion.6 = bf16[360,16384]{1,0:T(8,128)(2,1)} fusion(f32[16384,360]{0,1:T(8,128)} %get-tuple-element.48, bf16[360,90]{0,1:T(8,128)(2,1)S(1)} %copy-done.8, bf16[90,16384]{1,0:T(8,128)(2,1)S(1)} %bitcast.166), kind=kOutput, calls=%fused_computation.16 | convolution fusion | flops 1173749760 | bytes 38403360 | tf_op jit(solution)/shard_map/dot_general | solution.py:75
  428.6 8.7 %convolution_multiply_fusion.1 = f32[90,360]{1,0:T(8,128)} fusion(bf16[360,16384]{1,0:T(8,128)(2,1)} %fusion.6, f32[90,16384]{1,0:T(8,128)S(1)} %bitcast.152, f32[90]{0:T(128)S(1)} %copy-done.15, f32[90]{0:T(128)S(1)} %copy-done.10, f32[16384]{0:T(1024)S(1)} %bitcast.172, f32[16384]{0:T(1024)S(1)} %bitcast.176), kind=kOutput, calls=%fused_computation.48 | convolution fusion | flops 1069088384 | bytes 17956112 | tf_op jit(solution)/shard_map/dot_general | solution.py:41
  437.3 10.5 %fusion.13 = (f32[16384]{0:T(1024)S(1)}, f32[16384,90]{0,1:T(8,128)}) fusion(f32[90,16384]{1,0:T(8,128)S(1)} %bitcast.153, f32[16384]{0:T(1024)S(1)} %bitcast.173, f32[16384]{0:T(1024)S(1)} %bitcast.177, f32[90]{0:T(128)S(1)} %copy-done.10, bf16[360,16384]{1,0:T(8,128)(2,1)} %fusion.6, bf16[90,360]{1,0:T(8,128)(2,1)S(1)} %copy-done.7), kind=kOutput, calls=%fused_computation.31 | convolution fusion | flops 1069039616 | bytes 23854728 | tf_op jit(solution)/shard_map/dot_general | solution.py:78
  447.8 8.6 %convolution_multiply_fusion.2 = f32[360,90]{0,1:T(8,128)} fusion(bf16[360,16384]{1,0:T(8,128)(2,1)} %get-tuple-element.47, bf16[90,16384]{1,0:T(8,128)(2,1)S(1)} %bitcast.167), kind=kOutput, calls=%fused_computation.49 | convolution fusion | flops 1061715584 | bytes 14875200 | tf_op jit(solution)/shard_map/dot_general | solution.py:41
  456.4 6.9 %fusion.10 = bf16[90,16384]{1,0:T(8,128)(2,1)S(1)} fusion(bf16[360,16384]{1,0:T(8,128)(2,1)} %get-tuple-element.47, bf16[360,90]{0,1:T(8,128)(2,1)S(1)} %copy-done.8, bf16[16384,90]{0,1:T(8,128)(2,1)S(1)} %fusion.7, f32[90]{0:T(128)S(1)} %copy-done.11), kind=kOutput, calls=%fused_computation.26 | convolution fusion | flops 1067581440 | bytes 17759880 | tf_op jit(solution)/shard_map/dot_general | solution.py:68
  463.3 1.7 copy.117
  465.0 2.0 slice_bitcast_fusion
  467.0 3.2 reduce_sum.132
  470.2 6.2 fusion.12
  476.4 7.0 %copy.119 = f32[12,8,32,512]{3,2,1,0:T(8,128)} copy(f32[12,8,32,512]{3,1,2,0:T(8,128)S(1)} %bitcast.159) | data formatting | bytes 12582912
  483.4 31.8 %multiply_reduce_fusion = (f32[90]{0:T(128)S(1)}, f32[90]{0:T(128)S(1)}, f32[90]{0:T(128)S(1)}, f32[90]{0:T(128)S(1)}, f32[90]{0:T(128)S(1)}, /*index=5*/f32[90]...) fusion(f32[90,34,514]{2,1,0:T(8,128)} %maximum_convert_fusion, f32[96,32,512]{2,1,0:T(8,128)} %bitcast.160), kind=kLoop, calls=%fused_computation.34 | loop fusion | flops 26541270 | bytes 58985640 | tf_op jit(solution)/shard_map/reduce_sum | solution.py:90
  515.2 72.7 %psum.23 = f32[9,90]{1,0:T(8,128)} all-reduce(f32[9,90]{1,0:T(8,128)S(1)} %broadcast_multiply_fusion.3), channel_id=1, replica_groups=mesh['face'=8,'tile'=16] {'face','tile'}, use_global_device_ids=true, to_apply=%region_23.24 | all-reduce | flops 810 | bytes 6480 | tf_op jit(solution)/shard_map/psum | solution.py:211
  588.0 76.5 %all-reduce.4.cloned.1.call-done = (f32[90,360]{1,0:T(8,128)}, f32[360,90]{0,1:T(8,128)}) async-done(((f32[90,360]{1,0:T(8,128)}, f32[360,90]{0,1:T(8,128)}), (f32[90,360]{1,0:T(8,128)}, f32[360,90]{0,1:T(8,128)})) %all-reduce.4.cloned.1.call-update) | async-done | bytes 259216 | tf_op jit(solution)/shard_map/psum | solution.py:211
  664.5 1.6 copy.134
  666.1 1.6 copy.135
  (107 shorter events, 22.9 us)
Async XLA Ops:
  7.2 20.5 %copy-start = (bf16[64,16,128]{2,1,0:T(8,128)(2,1)S(1)}, bf16[64,16,128]{2,1,0:T(8,128)(2,1)}, u32[]{:S(2)}) copy-start(bf16[64,16,128]{2,1,0:T(8,128)(2,1)} %param.16) | copy-start | bytes 786436
  8.0 48.0 %copy-start.17 = (s32[128]{0:T(128)S(1)}, s32[128]{0:T(128)}, u32[]{:S(2)}) copy-start(s32[128]{0:T(128)} %param.20) | copy-start | bytes 1540
  15.5 30.7 %all-to-all-start.1 = ((s32[128,1,2]{2,1,0:T(1,128)}), s32[128,1,2]{2,1,0:T(1,128)S(1)}, u32[]{:S(2)}, u32[]{:S(2)}) async-start(s32[128,1,2]{2,1,0:T(1,128)} %copy.85), calls=%async_computation.1 | async-start | bytes 131072 | tf_op jit(solution)/shard_map/all_to_all | solution.py:156
  46.2 28.7 %all-to-all-start.2 = ((bf16[128,2,16,128]{3,2,1,0:T(8,128)(2,1)}), bf16[128,2,16,128]{3,2,1,0:T(8,128)(2,1)S(1)}, u32[]{:S(2)}, u32[]{:S(2)}) async-start(bf16[128,2,16,128]{3,2,1,0:T(8,128)(2,1)} %scatter_fusion.1), calls=%async_computation.2 | async-start | bytes 2097152 | tf_op jit(solution)/shard_map/all_to_all | solution.py:155
  74.9 28.2 %all-to-all-start = ((s32[128,1,1]{2,1,0:T(1,128)}), s32[128,1,1]{2,1,0:T(1,128)S(1)}, u32[]{:S(2)}, u32[]{:S(2)}) async-start(s32[128,1,1]{2,1,0:T(1,128)} %copy.84), calls=%async_computation | async-start | bytes 131072 | tf_op jit(solution)/shard_map/all_to_all | solution.py:169
  79.8 60.8 %copy-start.12 = (bf16[16,90]{1,0:T(8,128)(2,1)S(1)}, bf16[16,90]{1,0:T(8,128)(2,1)}, u32[]{:S(2)}) copy-start(bf16[16,90]{1,0:T(8,128)(2,1)} %param.22) | copy-start | bytes 8644
  79.8 60.8 %copy-start.14 = (f32[90]{0:T(128)S(1)}, f32[90]{0:T(128)}, u32[]{:S(2)}) copy-start(f32[90]{0:T(128)} %param.23) | copy-start | bytes 1084
  103.1 23.4 %all-to-all-start.3 = ((bf16[128,16,128]{2,1,0:T(8,128)(2,1)}), bf16[128,16,128]{2,1,0:T(8,128)(2,1)S(1)}, u32[]{:S(2)}, u32[]{:S(2)}) async-start(bf16[128,16,128]{2,1,0:T(8,128)(2,1)} %scatter_fusion.3), calls=%async_computation.3 | async-start | bytes 1048576 | tf_op jit(solution)/shard_map/all_to_all | solution.py:168
  113.0 77.6 %all-gather.3.cloned.1.call-start = ((), (), s32[]{:S(2)}) async-start(), calls=%async_computation.5 | async-start | bytes 1566720 | tf_op jit(solution)/shard_map/all_gather | solution.py:179
  143.9 1.7 copy-start.3
  259.0 10.6 %copy-start.9 = (s32[8,4,3]{0,1,2:T(4,128)S(1)}, s32[8,4,3]{0,1,2:T(4,128)}, u32[]{:S(2)}) copy-start(s32[8,4,3]{0,1,2:T(4,128)} %param.21) | copy-start | bytes 1156
  265.1 40.8 %all-to-all-start.4 = ((bf16[8,2,92160]{2,1,0:T(2,128)(2,1)}), bf16[8,2,92160]{2,1,0:T(2,128)(2,1)}, u32[]{:S(2)}, u32[]{:S(2)}) async-start(bf16[8,2,92160]{2,1,0:T(2,128)(2,1)} %reshape.303), calls=%async_computation.4 | async-start | bytes 5898240 | tf_op jit(solution)/shard_map/all_to_all | solution.py:187
  269.6 6.7 copy-start.13
  269.6 394.9 %all-reduce.4.cloned.1.call-start = ((), (), s32[]{:S(2)}) async-start(), calls=%async_computation.6 | async-start | bytes 589824 | tf_op jit(solution)/shard_map/psum | solution.py:211
  280.1 56.4 %collective-permute-start = (bf16[90,1,512]{2,0,1:T(8,128)(2,1)}, bf16[90,1,512]{2,0,1:T(8,128)(2,1)S(1)}, u32[]{:S(2)}, u32[]{:S(2)}) collective-permute-start(bf16[90,1,512]{2,0,1:T(8,128)(2,1)} %get-tuple-element.18), channel_id=1, source_target_pairs={{0,1},{1,2},{2,3},{3,4},{4,5},{5,6},{6,7},{7,8},{8,9},{9,10},{10,1... | collective-permute-start | bytes 276488 | tf_op jit(solution)/shard_map/ppermute | solution.py:21
  283.1 53.5 %collective-permute-start.1 = (bf16[90,1,512]{2,0,1:T(8,128)(2,1)}, bf16[90,1,512]{2,0,1:T(8,128)(2,1)}, u32[]{:S(2)}, u32[]{:S(2)}) collective-permute-start(bf16[90,1,512]{2,0,1:T(8,128)(2,1)} %get-tuple-element.19), channel_id=1, source_target_pairs={{1,0},{2,1},{3,2},{4,3},{5,4},{6,5},{7,6},{8,7},{9,8},{10,9},{11,1... | collective-permute-start | bytes 276488 | tf_op jit(solution)/shard_map/ppermute | solution.py:23
  334.0 0.8 copy-start.6
  383.8 8.0 %slice-start = ((s8[5898240]{0:T(1024)(128)(4,1)}), s8[4194304]{0:T(1024)(128)(4,1)S(1)}, s32[]{:S(2)}) async-start(s8[5898240]{0:T(1024)(128)(4,1)} %bitcast.155), calls=%async_computation.7 | async-start | bytes 8388608
  387.4 4.5 slice-start.1
  391.7 45.6 %copy-start.2 = (f32[12,8,32,512]{3,1,2,0:T(8,128)}, f32[12,8,32,512]{3,1,2,0:T(8,128)S(1)}, u32[]{:S(2)}) copy-start(f32[12,8,32,512]{3,1,2,0:T(8,128)S(1)} %copy.114) | copy-start | bytes 18874372
  391.7 1.0 copy-start.7
  391.7 0.9 copy-start.10
  391.8 0.9 copy-start.15
  391.8 0.9 copy-start.16
  392.7 15.2 %copy-start.4 = (bf16[12,8,32,512]{3,1,2,0:T(8,128)(2,1)S(1)}, bf16[12,8,32,512]{3,1,2,0:T(8,128)(2,1)}, u32[]{:S(2)}) copy-start(bf16[12,8,32,512]{3,1,2,0:T(8,128)(2,1)} %copy.118) | copy-start | bytes 9437188
  392.7 15.2 %copy-start.8 = (bf16[360,90]{0,1:T(8,128)(2,1)S(1)}, bf16[360,90]{0,1:T(8,128)(2,1)}, u32[]{:S(2)}) copy-start(bf16[360,90]{0,1:T(8,128)(2,1)} %param.29) | copy-start | bytes 194404
  437.3 10.6 %copy-start.5 = (bf16[12,8,32,512]{3,1,2,0:T(8,128)(2,1)S(1)}, bf16[12,8,32,512]{3,1,2,0:T(8,128)(2,1)}, u32[]{:S(2)}) copy-start(bf16[12,8,32,512]{3,1,2,0:T(8,128)(2,1)} %copy.118) | copy-start | bytes 9437188
  447.8 8.6 %copy-start.11 = (f32[90]{0:T(128)S(1)}, f32[90]{0:T(128)}, u32[]{:S(2)}) copy-start(f32[90]{0:T(128)} %param.30) | copy-start | bytes 1084
  483.3 184.3 %copy-start.1 = (bf16[64,16,128]{2,1,0:T(8,128)(2,1)S(1)}, bf16[64,16,128]{2,1,0:T(8,128)(2,1)}, u32[]{:S(2)}) copy-start(bf16[64,16,128]{2,1,0:T(8,128)(2,1)} %param.16) | copy-start | bytes 786436
Sparse Core Ops, SparseCore 0:
  147.4 43.0 all-gather.2
  515.3 149.1 all-reduce.3
